TPU v7x, 32 devices: a whole 2x2x4 slice. The times are simulated.
32 devices in a mesh: freq: 2 (over y), sub: 16 (over z, x, core).
Axes of the slice: x: 2, y: 2, z: 4, core: 2. Of those that a mesh axis runs over, the one named last changes fastest.
Arguments:
- tri_xyz: float32 [3, 8192], P(None, 'sub'), may hold values from -1 to 1
- leaf_tri: int32 [32, 256], P('sub'), may hold values from 0 to 511, as said below
- leaf_proxy: int32 [32, 1024], P('sub'), may hold values from 0 to 8191
- node_proxy: int32 [16, 1024], P('sub'), may hold values from 0 to 8191
- mid_proxy: int32 [2, 1024], replicated, may hold values from 0 to 8191
- root_proxy: int32 [1024], replicated, may hold values from 0 to 8191
- level1_pos: int32 [16], P('sub'), may hold values from 0 to 7, as said below
- kappa: float32 [2], P('freq'), parts along dimension 0, may hold values from 20 to 40
- omega: float32 [2048, 128], replicated, may hold values from -0.125 to 0.125
Outputs:
- leaf_basis: float32 [64, 256, 128], P(('freq', 'sub')), parts along dimension 0
- node_transfer: float32 [32, 256, 128], P(('freq', 'sub')), parts along dimension 0
- mid_transfer: float32 [32, 128, 128], P(('freq', 'sub')), parts along dimension 0
- root_transfer: float32 [32, 16, 128], P(('freq', 'sub')), parts along dimension 0
There are 2 independent parts, one for each index of `freq`. A program takes and returns all parts, laid end to end along the dimension named above; an argument that names none is the same for every part. Nothing has to cross between parts.
Inputs may be any that keep to these rules, and one draw needn't show every extreme that they name: `leaf_tri`: the 2 leaves of one level-one cluster name each of its 512 triangles once. `level1_pos`: each aligned block of 8 entries is a permutation.
All inputs are finite; a program needn't handle non-finite values.
Results may differ from a plain program's by a relative error of at most 0.04.
Values sent between devices are 32-bit elements; how exact they have to be, the bound alone decides.
A program may use at most 128 MiB of HBM per device.

v0:
```python
import functools
import math

import jax
import jax.numpy as jnp
from jax import lax
from jax.experimental import pallas as pl
from jax.experimental.pallas import tpu as pltpu
from jax.sharding import PartitionSpec as P

GROUP = 8
LANES = 128
ROWS8 = 8
ROW_CHUNK = 128
soft_sq = 0.0025
MESH = pl.DeviceIdType.MESH
F32 = jnp.float32
BF16 = jnp.bfloat16

SIN_COEF = (
    3.141592640130707,
    -5.167710083507899,
    2.5500775232144695,
    -0.5982912856189484,
    0.07765766030176967,
)
COS_COEF = (
    1.9999999064952165,
    -9.8695856612393,
    8.116822705725152,
    -2.6637531361606688,
    0.43937922219243786,
)


def split(block):
    high = block.astype(BF16)
    return high, (block - high.astype(F32)).astype(BF16)


def dot3(left, right, dims):
    left_high, left_low = split(left)
    right_high, right_low = split(right)
    dot = functools.partial(
        lax.dot_general, dimension_numbers=(dims, ((), ())), preferred_element_type=F32
    )
    return dot(left_high, right_high) + (dot(left_high, right_low) + dot(left_low, right_high))


def mul_nn(left, right):
    return dot3(left, right, ((1,), (0,)))


def mul_nt(left, right):
    return dot3(left, right, ((1,), (1,)))


def mul_tn(left, right):
    return dot3(left, right, ((0,), (0,)))


def inverse_factors(grams):
    size = grams[0].shape[0]
    lane = lax.broadcasted_iota(jnp.int32, (ROWS8, size), 1)
    sub = lax.broadcasted_iota(jnp.int32, (ROWS8, size), 0)
    states = list(grams)
    done = [[] for _ in grams]
    for start in range(0, size, ROWS8):
        stop = start + ROWS8
        in_panel = (lane >= start) & (lane < stop)
        unit = (lane - start == sub).astype(F32)
        for which, state in enumerate(states):
            panel = state[:ROWS8]
            entry = {}
            for col in range(ROWS8):
                column = jnp.broadcast_to(panel[:, start + col : start + col + 1], (ROWS8, size))
                for row in range(col, ROWS8):
                    entry[row, col] = jnp.broadcast_to(column[row : row + 1], (ROWS8, size))
            right = jnp.where(in_panel, unit, panel)
            lines = [jnp.broadcast_to(right[row : row + 1], (ROWS8, size)) for row in range(ROWS8)]
            for k in range(ROWS8):
                scale = lax.rsqrt(entry[k, k])
                lines[k] = lines[k] * scale
                for row in range(k + 1, ROWS8):
                    entry[row, k] = entry[row, k] * scale
                for row in range(k + 1, ROWS8):
                    lines[row] = lines[row] - entry[row, k] * lines[k]
                    for col in range(k + 1, row + 1):
                        entry[row, col] = entry[row, col] - entry[row, k] * entry[col, k]
            solved = lines[0]
            for k in range(1, ROWS8):
                solved = jnp.where(sub == k, lines[k], solved)
            done[which].append(jnp.where(lane < stop, solved, 0.0))
            if stop < size:
                high, low = split(solved)
                high_f, low_f = high.astype(F32), low.astype(F32)
                left = jnp.concatenate([high_f, low_f, high_f, jnp.zeros_like(high_f)], axis=0)
                right = jnp.concatenate([high_f, high_f, low_f, jnp.zeros_like(high_f)], axis=0)
                update = lax.dot_general(
                    left.T[stop:].astype(BF16),
                    right.astype(BF16),
                    (((1,), (0,)), ((), ())),
                    preferred_element_type=F32,
                )
                rest = state[ROWS8:]
                rest_lane = lax.broadcasted_iota(jnp.int32, rest.shape, 1)
                rest = jnp.where((rest_lane >= start) & (rest_lane < stop), 0.0, rest)
                states[which] = rest - update
    return [jnp.concatenate(rows, axis=0) for rows in done]


def gather_kernel(count, own_ref, table_ref, send_sem, recv_sem, local_sem):
    me = lax.axis_index("sub")
    barrier = pltpu.get_barrier_semaphore()

    def greet(step, carry):
        pl.semaphore_signal(
            barrier, inc=1, device_id={"sub": lax.rem(me + step, count)}, device_id_type=MESH
        )
        return carry

    lax.fori_loop(1, count, greet, 0)
    local = pltpu.make_async_copy(own_ref, table_ref.at[:, me], local_sem)
    local.start()
    pl.semaphore_wait(barrier, count - 1)

    def copy_of(step):
        return pltpu.make_async_remote_copy(
            src_ref=own_ref,
            dst_ref=table_ref.at[:, me],
            send_sem=send_sem.at[step],
            recv_sem=recv_sem.at[step],
            device_id={"sub": lax.rem(me + step, count)},
            device_id_type=MESH,
        )

    def start(step, carry):
        copy_of(step).start()
        return carry

    def finish(step, carry):
        copy_of(step).wait()
        return carry

    lax.fori_loop(1, count, start, 0)
    local.wait()
    lax.fori_loop(1, count, finish, 0)


def leaf_kernel(
    per_dev,
    kappa_ref,
    table_ref,
    leaf_tri_ref,
    leaf_proxy_ref,
    node_proxy_ref,
    mid_proxy_ref,
    root_proxy_ref,
    omega_ref,
    basis_ref,
    transfer_ref,
    coef_ref,
    sums_ref,
    cols_ref,
    rows_ref,
    weight_ref,
    high_ref,
    low_ref,
    sketch_ref,
):
    device = lax.axis_index("sub")
    leaves, leaf_rows = leaf_tri_ref.shape
    proxies = leaf_proxy_ref.shape[1]
    rank = omega_ref.shape[1]
    rows = leaves * leaf_rows

    pieces = []
    for axis in range(3):
        turned = table_ref[axis].T
        first = turned.astype(BF16)
        left = turned - first.astype(F32)
        second = left.astype(BF16)
        third = (left - second.astype(F32)).astype(BF16)
        pieces.append((first, second, third))
    blocks = table_ref.shape[1]

    def centroids(index):
        width = index.shape[1]
        within = index % per_dev
        block = (index // per_dev) * ROWS8 + within // LANES
        place = within % LANES
        hot = jnp.where(
            lax.broadcasted_iota(jnp.int32, (blocks, width), 0) == block, 1.0, 0.0
        ).astype(BF16)
        chosen = lax.broadcasted_iota(jnp.int32, (LANES, width), 0) == place
        found = []
        for axis in range(3):
            wide = None
            for piece in pieces[axis]:
                term = jnp.dot(piece, hot, preferred_element_type=F32)
                wide = term if wide is None else wide + term
            found.append(jnp.sum(jnp.where(chosen, wide, 0.0), axis=0, keepdims=True))
        return found

    group = device // GROUP
    sets = [leaf_proxy_ref[leaf : leaf + 1, :] for leaf in range(leaves)]
    sets += [node_proxy_ref[...], mid_proxy_ref[pl.ds(group, 1), :], root_proxy_ref[...]]
    for number, index in enumerate(sets):
        found = centroids(index)
        for axis in range(3):
            cols_ref[number, axis : axis + 1, :] = found[axis]
    for leaf in range(leaves):
        found = centroids(leaf_tri_ref[leaf : leaf + 1, :] + device * per_dev)
        turned = jnp.concatenate(found + [jnp.zeros((ROWS8 - 3, leaf_rows), F32)], axis=0).T
        for axis in range(3):
            rows_ref[axis, leaf * leaf_rows : (leaf + 1) * leaf_rows, :] = jnp.broadcast_to(
                turned[:, axis : axis + 1], (leaf_rows, rows_ref.shape[2])
            )

    omega_high, omega_low = split(omega_ref[...])
    weight_ref[:, :rank] = omega_high
    weight_ref[:, rank:] = omega_low

    turns = kappa_ref[0] * (0.5 / math.pi)
    chunks = rows // ROW_CHUNK
    per_leaf = leaf_rows // ROW_CHUNK
    width = rows_ref.shape[2]

    def poly(coef, value):
        total = jnp.full_like(value, coef[-1])
        for number in coef[-2::-1]:
            total = total * value + number
        return total

    def sketches(step, carry):
        level = step // chunks
        chunk = step % chunks
        number = jnp.where(level == 0, chunk // per_leaf, level + leaves - 1)
        base = pl.multiple_of(chunk * ROW_CHUNK, ROW_CHUNK)
        for top in range(0, ROW_CHUNK, 16):
            mine = [rows_ref[axis, pl.ds(base + top, 16), :] for axis in range(3)]
            for begin in range(0, proxies, width):
                squared = None
                for axis in range(3):
                    apart = mine[axis] - cols_ref[number, axis : axis + 1, begin : begin + width]
                    squared = apart * apart if squared is None else squared + apart * apart
                squared = squared + soft_sq
                inverse = lax.rsqrt(squared)
                phase = (squared * inverse) * turns
                phase = phase - jnp.round(phase)
                square = phase * phase
                sine = phase * poly(SIN_COEF, square)
                twice = poly(COS_COEF, square)
                imag = (sine * twice) * inverse
                sine = sine * sine
                real = (1.0 - (sine + sine)) * inverse
                for value, offset in ((real, 0), (imag, proxies)):
                    high, low = split(value)
                    high_ref[top : top + 16, offset + begin : offset + begin + width] = high
                    low_ref[top : top + 16, offset + begin : offset + begin + width] = low
        wide = jnp.dot(high_ref[...], weight_ref[...], preferred_element_type=F32)
        fine = jnp.dot(low_ref[...], weight_ref[:, :rank], preferred_element_type=F32)
        sketch_ref[level, pl.ds(base, ROW_CHUNK), :] = wide[:, :rank] + (wide[:, rank:] + fine)
        return carry

    lax.fori_loop(0, 4 * chunks, sketches, 0)

    own = [sketch_ref[0, leaf * leaf_rows : (leaf + 1) * leaf_rows, :] for leaf in range(leaves)]
    factors = inverse_factors([mul_tn(block, block) for block in own])
    upward = []
    for leaf in range(leaves):
        basis = mul_nt(own[leaf], factors[leaf])
        basis_ref[leaf] = basis
        far = jnp.concatenate(
            [sketch_ref[k, leaf * leaf_rows : (leaf + 1) * leaf_rows, :] for k in (1, 2, 3)], axis=1
        )
        upward.append(mul_tn(basis, far))
    stacked = jnp.concatenate(upward, axis=0)
    first = stacked[:, :rank]
    (factor,) = inverse_factors([mul_tn(first, first)])
    transfer = mul_nt(first, factor)
    transfer_ref[...] = transfer
    coefs = mul_tn(transfer, stacked[:, rank:])
    coef_ref[...] = coefs[:, :rank]
    sums = mul_tn(coefs[:, :rank], coefs)
    sums_ref[:rank] = sums[:, :rank]
    sums_ref[rank:] = sums[:, rank:]


def tree_kernel(
    mids,
    pos_ref,
    coef_ref,
    sums_ref,
    mid_ref,
    root_ref,
    part_ref,
    full_ref,
    own_ref,
    other_ref,
    part_send,
    part_recv,
    full_send,
    full_recv,
    root_send,
    root_recv,
):
    rank = coef_ref.shape[0]
    count = mids * GROUP
    me = lax.axis_index("sub")
    member = lax.rem(me, GROUP)
    first = me - member
    share = sums_ref.shape[0] // GROUP

    def sibling(step):
        return first + lax.rem(member + step, GROUP)

    def cousin(step):
        return lax.rem(me + step * GROUP, count)

    barrier = pltpu.get_barrier_semaphore()
    for step in range(1, GROUP):
        pl.semaphore_signal(
            barrier, inc=1, device_id={"sub": sibling(step)}, device_id_type=MESH
        )
    for step in range(1, mids):
        pl.semaphore_signal(barrier, inc=1, device_id={"sub": cousin(step)}, device_id_type=MESH)
    pl.semaphore_wait(barrier, GROUP - 1 + mids - 1)

    copies = []
    for step in range(1, GROUP):
        begin = pl.multiple_of(lax.rem(member + step, GROUP) * share, share)
        copy = pltpu.make_async_remote_copy(
            src_ref=sums_ref.at[pl.ds(begin, share)],
            dst_ref=part_ref.at[step],
            send_sem=part_send.at[step],
            recv_sem=part_recv.at[step],
            device_id={"sub": sibling(step)},
            device_id_type=MESH,
        )
        copy.start()
        copies.append(copy)
    begin = pl.multiple_of(member * share, share)
    total = sums_ref[pl.ds(begin, share), :]
    for step, copy in enumerate(copies, 1):
        copy.wait()
        total = total + part_ref[step]
    full_ref[pl.ds(begin, share), :] = total
    copies = []
    for step in range(1, GROUP):
        copy = pltpu.make_async_remote_copy(
            src_ref=full_ref.at[pl.ds(begin, share)],
            dst_ref=full_ref.at[pl.ds(begin, share)],
            send_sem=full_send.at[step],
            recv_sem=full_recv.at[step],
            device_id={"sub": sibling(step)},
            device_id_type=MESH,
        )
        copy.start()
        copies.append(copy)
    for copy in copies:
        copy.wait()

    (factor,) = inverse_factors([full_ref[:rank]])
    own = mul_nn(factor, full_ref[rank:])
    own_ref[...] = own
    copies = []
    for step in range(1, mids):
        copy = pltpu.make_async_remote_copy(
            src_ref=own_ref,
            dst_ref=other_ref.at[step],
            send_sem=root_send.at[step],
            recv_sem=root_recv.at[step],
            device_id={"sub": cousin(step)},
            device_id_type=MESH,
        )
        copy.start()
        copies.append(copy)
    mid_ref[...] = mul_nt(coef_ref[...], factor)
    gram = mul_tn(own, own)
    for step, copy in enumerate(copies, 1):
        copy.wait()
        other = other_ref[step]
        gram = gram + mul_tn(other, other)
    (factor,) = inverse_factors([gram])
    share_rows = rank // GROUP
    mine = jnp.zeros((share_rows, rank), F32)
    for place in range(GROUP):
        block = own[place * share_rows : (place + 1) * share_rows]
        mine = jnp.where(pos_ref[...] == place, block, mine)
    root_ref[...] = mul_nt(mine, factor)


def on_device(
    tri_xyz, leaf_tri, leaf_proxy, node_proxy, mid_proxy, root_proxy, level1_pos, kappa, omega
):
    count = lax.axis_size("sub")
    mids = count // GROUP
    per_dev = tri_xyz.shape[1]
    leaves, leaf_rows = leaf_tri.shape
    proxies = leaf_proxy.shape[1]
    rank = omega.shape[1]
    vmem = pl.BlockSpec(memory_space=pltpu.VMEM)
    smem = pl.BlockSpec(memory_space=pltpu.SMEM)
    dma = pltpu.SemaphoreType.DMA
    limit = 48 * 1024 * 1024

    own = tri_xyz.reshape(3, per_dev // LANES, LANES)
    own = jnp.pad(own, ((0, 0), (0, ROWS8 - per_dev // LANES), (0, 0)))
    table = pl.pallas_call(
        functools.partial(gather_kernel, count),
        out_shape=jax.ShapeDtypeStruct((3, count, ROWS8, LANES), F32),
        in_specs=[vmem],
        out_specs=vmem,
        scratch_shapes=[dma((count,)), dma((count,)), dma],
        compiler_params=pltpu.CompilerParams(
            collective_id=0, has_side_effects=True, vmem_limit_bytes=limit
        ),
        name="gather_centroids",
    )(own)
    table = table.reshape(3, count * ROWS8, LANES)

    basis, transfer, coef, sums = pl.pallas_call(
        functools.partial(leaf_kernel, per_dev),
        out_shape=(
            jax.ShapeDtypeStruct((leaves, leaf_rows, rank), F32),
            jax.ShapeDtypeStruct((leaves * rank, rank), F32),
            jax.ShapeDtypeStruct((rank, rank), F32),
            jax.ShapeDtypeStruct((2 * rank, rank), F32),
        ),
        in_specs=[smem] + [vmem] * 7,
        out_specs=(vmem,) * 4,
        scratch_shapes=[
            pltpu.VMEM((leaves + 3, ROWS8, proxies), F32),
            pltpu.VMEM((3, leaves * leaf_rows, 2 * LANES), F32),
            pltpu.VMEM((2 * proxies, 2 * rank), BF16),
            pltpu.VMEM((ROW_CHUNK, 2 * proxies), BF16),
            pltpu.VMEM((ROW_CHUNK, 2 * proxies), BF16),
            pltpu.VMEM((4, leaves * leaf_rows, rank), F32),
        ],
        compiler_params=pltpu.CompilerParams(vmem_limit_bytes=limit),
        name="leaf_and_node",
    )(kappa, table, leaf_tri, leaf_proxy, node_proxy, mid_proxy, root_proxy[None], omega)

    share = 2 * rank // GROUP
    mid, root = pl.pallas_call(
        functools.partial(tree_kernel, mids),
        out_shape=(
            jax.ShapeDtypeStruct((rank, rank), F32),
            jax.ShapeDtypeStruct((rank // GROUP, rank), F32),
        ),
        in_specs=[vmem, vmem, vmem],
        out_specs=(vmem, vmem),
        scratch_shapes=[
            pltpu.VMEM((GROUP, share, rank), F32),
            pltpu.VMEM((2 * rank, rank), F32),
            pltpu.VMEM((rank, rank), F32),
            pltpu.VMEM((mids, rank, rank), F32),
            dma((GROUP,)),
            dma((GROUP,)),
            dma((GROUP,)),
            dma((GROUP,)),
            dma((mids,)),
            dma((mids,)),
        ],
        compiler_params=pltpu.CompilerParams(
            collective_id=1, has_side_effects=True, vmem_limit_bytes=limit
        ),
        name="mid_and_root",
    )(jnp.broadcast_to(level1_pos[0], (rank // GROUP, rank)), coef, sums)
    return (basis, transfer[None], mid[None], root[None])


def solution(mesh):
    in_specs = (
        P(None, "sub"),
        P("sub", None),
        P("sub", None),
        P("sub", None),
        P(),
        P(),
        P("sub"),
        P("freq"),
        P(),
    )
    out_specs = (
        P(("freq", "sub"), None, None),
        P(("freq", "sub"), None, None),
        P(("freq", "sub"), None, None),
        P(("freq", "sub"), None, None),
    )
    return jax.shard_map(
        on_device, mesh=mesh, in_specs=in_specs, out_specs=out_specs, check_vma=False
    )
```

profile of v0, /device:TPU:0, one launch (start us, length us, event | category | flops | bytes accessed | tf_op | source)
XLA Modules:
  0.0 81.5 jit_solution(4382180696428101530)
XLA Ops:
  0.6 0.7 reshape.14
  1.4 0.0 copy-start.1
  1.4 0.0 copy-start.2
  1.4 0.0 copy-start.4
  1.4 0.0 copy-start.5
  1.4 10.4 %gather_centroids.1 = f32[3,16,8,128]{3,2,1,0:T(8,128)S(1)} custom-call(f32[3,8,128]{2,1,0:T(8,128)S(1)} %pad.4.own_ref), custom_call_target="tpu_custom_call" | custom-call | tf_op jit(solution)/shard_map/gather_centroids/pallas_call | solution.py:410
  11.8 0.0 copy-start.3
  12.5 0.0 copy-done.1
  12.5 0.0 copy-done.2
  12.5 0.0 copy-done.4
  12.5 0.0 copy-done.5
  12.5 0.0 copy-done.3
  12.6 0.0 copy-start
  12.6 1.2 %copy-done = f32[2048,128]{1,0:T(8,128)S(1)} copy-done((f32[2048,128]{1,0:T(8,128)S(1)}, f32[2048,128]{1,0:T(8,128)}, u32[]{:S(2)}) %copy-start) | copy-done | bytes 1048600
  13.8 35.9 %leaf_and_node.1 = (f32[2,256,128]{2,1,0:T(8,128)}, f32[256,128]{1,0:T(8,128)}, f32[128,128]{1,0:T(8,128)S(1)}, f32[256,128]{1,0:T(8,128)S(1)}) custom-call(f32[1]{0:T(128)S(6)} %copy.16.kappa_ref, f32[3,128,128]{2,1,0:T(8,128)S(1)} %bitcast.7, s32[2,256]{1,0:T(2,128)S(1)} %copy-done.5, s32[2,1024]{1,0:T(2,128)S(1)} %copy-done.1, s32[1,1024]{1,0:T(1,128)S(1)} %copy-done.3, ...), custom_call_target="tpu_custom_call" | custom-call | tf_op jit(solution)/shard_map/leaf_and_node/pallas_call | solution.py:423
  50.4 29.8 %mid_and_root.1 = (f32[128,128]{1,0:T(8,128)S(1)}, f32[16,128]{1,0:T(8,128)S(1)}) custom-call(s32[16,128]{1,0:T(8,128)S(1)} %broadcast_in_dim.17.pos_ref, f32[128,128]{1,0:T(8,128)S(1)} %get-tuple-element.12.coef_ref, f32[256,128]{1,0:T(8,128)S(1)} %get-tuple-element.13.sums_ref), custom_call_target="tpu_custom_call" | custom-call | tf_op jit(solution)/shard_map/mid_and_root/pallas_call | solution.py:446
  80.2 0.6 copy.17
  80.9 0.6 copy.18
  (2 shorter events, 0.0 us)
Async XLA Ops:
  1.4 11.2 %copy-start.1 = (s32[2,1024]{1,0:T(2,128)S(1)}, s32[2,1024]{1,0:T(2,128)}, u32[]{:S(2)}) copy-start(s32[2,1024]{1,0:T(2,128)} %leaf_proxy_ref.1) | copy-start | bytes 24580
  1.4 11.2 %copy-start.2 = (s32[2,1024]{1,0:T(2,128)S(1)}, s32[2,1024]{1,0:T(2,128)}, u32[]{:S(2)}) copy-start(s32[2,1024]{1,0:T(2,128)} %mid_proxy_ref.1) | copy-start | bytes 24580
  1.4 11.2 %copy-start.4 = (s32[1024]{0:T(1024)S(1)}, s32[1024]{0:T(1024)}, u32[]{:S(2)}) copy-start(s32[1024]{0:T(1024)} %param.14) | copy-start | bytes 12292
  1.4 11.2 %copy-start.5 = (s32[2,256]{1,0:T(2,128)S(1)}, s32[2,256]{1,0:T(2,128)}, u32[]{:S(2)}) copy-start(s32[2,256]{1,0:T(2,128)} %leaf_tri_ref.1) | copy-start | bytes 6148
  11.8 0.7 copy-start.3
  12.6 1.2 %copy-start = (f32[2048,128]{1,0:T(8,128)S(1)}, f32[2048,128]{1,0:T(8,128)}, u32[]{:S(2)}) copy-start(f32[2048,128]{1,0:T(8,128)} %omega_ref.1) | copy-start | bytes 3145732
where the time goes:
time: 81.7 us; the launch traced here: 81.5 us
  Pallas kernels  76.2 us (93%)
  local copies, waits for them, and re-layouts  3.2 us (4%)
  between operations  2.05 us (3%)
    pallas_call x1, Pallas kernels, on_device(): pl.pallas_call(functools.partial(leaf_kernel, per_dev), out_shape=(jax.Sh...  35.9 us
    pallas_call x1, Pallas kernels, on_device(): pl.pallas_call(functools.partial(tree_kernel, mids), out_shape=(jax.Shape...  29.8 us
    pallas_call x1, Pallas kernels, on_device(): pl.pallas_call(functools.partial(gather_kernel, count), out_shape=jax.Sha...  10.4 us
    unnamed x14, local copies, waits for them, and re-layouts  2.48 us

commit v1 on v0

--- a/solution.py
+++ b/solution.py
@@ -59,53 +59,74 @@
     return dot3(left, right, ((0,), (0,)))
 
 
-def inverse_factors(grams):
+def inverse_factors(grams, scratch):
     size = grams[0].shape[0]
+    panels = size // ROWS8
     lane = lax.broadcasted_iota(jnp.int32, (ROWS8, size), 1)
     sub = lax.broadcasted_iota(jnp.int32, (ROWS8, size), 0)
-    states = list(grams)
+    states = [[gram[p * ROWS8 : (p + 1) * ROWS8] for p in range(panels)] for gram in grams]
     done = [[] for _ in grams]
-    for start in range(0, size, ROWS8):
-        stop = start + ROWS8
-        in_panel = (lane >= start) & (lane < stop)
+
+    def columns(block, start):
+        return [
+            jnp.broadcast_to(block[:, start + col : start + col + 1], (ROWS8, size))
+            for col in range(ROWS8)
+        ]
+
+    for number in range(panels):
+        start = number * ROWS8
+        in_panel = (lane >= start) & (lane < start + ROWS8)
         unit = (lane - start == sub).astype(F32)
-        for which, state in enumerate(states):
-            panel = state[:ROWS8]
+        for which, rows in enumerate(states):
+            panel = rows[number]
             entry = {}
-            for col in range(ROWS8):
-                column = jnp.broadcast_to(panel[:, start + col : start + col + 1], (ROWS8, size))
+            slot = scratch.at[which, number % 2]
+            for col, column in enumerate(columns(panel, start)):
+                slot[col] = column
                 for row in range(col, ROWS8):
-                    entry[row, col] = jnp.broadcast_to(column[row : row + 1], (ROWS8, size))
-            right = jnp.where(in_panel, unit, panel)
-            lines = [jnp.broadcast_to(right[row : row + 1], (ROWS8, size)) for row in range(ROWS8)]
+                    entry[row, col] = jnp.broadcast_to(slot[col, row : row + 1], (ROWS8, size))
+            slot[ROWS8] = jnp.where(in_panel, unit, panel)
+            lines = [
+                jnp.broadcast_to(slot[ROWS8, row : row + 1], (ROWS8, size)) for row in range(ROWS8)
+            ]
+            last = number + 1 == panels
+            if not last:
+                below = columns(rows[number + 1], start)
+                later = jnp.where(in_panel, 0.0, rows[number + 1])
             for k in range(ROWS8):
                 scale = lax.rsqrt(entry[k, k])
                 lines[k] = lines[k] * scale
                 for row in range(k + 1, ROWS8):
                     entry[row, k] = entry[row, k] * scale
+                if not last:
+                    below[k] = below[k] * scale
+                    later = later - below[k] * lines[k]
                 for row in range(k + 1, ROWS8):
-                    lines[row] = lines[row] - entry[row, k] * lines[k]
+                    factor = entry[row, k]
+                    lines[row] = lines[row] - factor * lines[k]
+                    if not last:
+                        below[row] = below[row] - factor * below[k]
                     for col in range(k + 1, row + 1):
-                        entry[row, col] = entry[row, col] - entry[row, k] * entry[col, k]
+                        entry[row, col] = entry[row, col] - factor * entry[col, k]
             solved = lines[0]
             for k in range(1, ROWS8):
                 solved = jnp.where(sub == k, lines[k], solved)
-            done[which].append(jnp.where(lane < stop, solved, 0.0))
-            if stop < size:
+            done[which].append(jnp.where(lane < start + ROWS8, solved, 0.0))
+            if not last:
+                rows[number + 1] = later
+            after = (number + 2) * ROWS8
+            if after < size:
                 high, low = split(solved)
                 high_f, low_f = high.astype(F32), low.astype(F32)
-                left = jnp.concatenate([high_f, low_f, high_f, jnp.zeros_like(high_f)], axis=0)
-                right = jnp.concatenate([high_f, high_f, low_f, jnp.zeros_like(high_f)], axis=0)
+                zero = jnp.zeros_like(high_f)
+                left = jnp.concatenate([high_f, low_f, high_f, zero], axis=0).astype(BF16)
+                right = jnp.concatenate([high_f, high_f, low_f, zero], axis=0).astype(BF16)
                 update = lax.dot_general(
-                    left.T[stop:].astype(BF16),
-                    right.astype(BF16),
-                    (((1,), (0,)), ((), ())),
-                    preferred_element_type=F32,
-                )
-                rest = state[ROWS8:]
-                rest_lane = lax.broadcasted_iota(jnp.int32, rest.shape, 1)
-                rest = jnp.where((rest_lane >= start) & (rest_lane < stop), 0.0, rest)
-                states[which] = rest - update
+                    left, right, (((0,), (0,)), ((), ())), preferred_element_type=F32
+                )[after:]
+                for p in range(number + 2, panels):
+                    begin = p * ROWS8 - after
+                    rows[p] = jnp.where(in_panel, 0.0, rows[p]) - update[begin : begin + ROWS8]
     return [jnp.concatenate(rows, axis=0) for rows in done]
 
 
@@ -166,7 +187,10 @@
     weight_ref,
     high_ref,
     low_ref,
+    high_too_ref,
+    low_too_ref,
     sketch_ref,
+    factor_ref,
 ):
     device = lax.axis_index("sub")
     leaves, leaf_rows = leaf_tri_ref.shape
@@ -232,7 +256,7 @@
             total = total * value + number
         return total
 
-    def sketches(step, carry):
+    def sample(step, slot):
         level = step // chunks
         chunk = step % chunks
         number = jnp.where(level == 0, chunk // per_leaf, level + leaves - 1)
@@ -256,17 +280,37 @@
                 real = (1.0 - (sine + sine)) * inverse
                 for value, offset in ((real, 0), (imag, proxies)):
                     high, low = split(value)
-                    high_ref[top : top + 16, offset + begin : offset + begin + width] = high
-                    low_ref[top : top + 16, offset + begin : offset + begin + width] = low
-        wide = jnp.dot(high_ref[...], weight_ref[...], preferred_element_type=F32)
-        fine = jnp.dot(low_ref[...], weight_ref[:, :rank], preferred_element_type=F32)
-        sketch_ref[level, pl.ds(base, ROW_CHUNK), :] = wide[:, :rank] + (wide[:, rank:] + fine)
+                    high_refs[slot][top : top + 16, offset + begin : offset + begin + width] = high
+                    low_refs[slot][top : top + 16, offset + begin : offset + begin + width] = low
+
+    def multiply(step, slot):
+        base = pl.multiple_of((step % chunks) * ROW_CHUNK, ROW_CHUNK)
+        wide = jnp.dot(high_refs[slot][...], weight_ref[...], preferred_element_type=F32)
+        fine = jnp.dot(low_refs[slot][...], weight_ref[:, :rank], preferred_element_type=F32)
+        sketch_ref[step // chunks, pl.ds(base, ROW_CHUNK), :] = wide[:, :rank] + (
+            wide[:, rank:] + fine
+        )
+
+    high_refs = (high_ref, high_too_ref)
+    low_refs = (low_ref, low_too_ref)
+    steps = 4 * chunks
+    sample(0, 0)
+
+    def pair(half, carry):
+        step = 2 * half
+        multiply(step, 0)
+        sample(step + 1, 1)
+        multiply(step + 1, 1)
+        sample(step + 2, 0)
         return carry
 
-    lax.fori_loop(0, 4 * chunks, sketches, 0)
+    lax.fori_loop(0, steps // 2 - 1, pair, 0)
+    multiply(steps - 2, 0)
+    sample(steps - 1, 1)
+    multiply(steps - 1, 1)
 
     own = [sketch_ref[0, leaf * leaf_rows : (leaf + 1) * leaf_rows, :] for leaf in range(leaves)]
-    factors = inverse_factors([mul_tn(block, block) for block in own])
+    factors = inverse_factors([mul_tn(block, block) for block in own], factor_ref)
     upward = []
     for leaf in range(leaves):
         basis = mul_nt(own[leaf], factors[leaf])
@@ -277,7 +321,7 @@
         upward.append(mul_tn(basis, far))
     stacked = jnp.concatenate(upward, axis=0)
     first = stacked[:, :rank]
-    (factor,) = inverse_factors([mul_tn(first, first)])
+    (factor,) = inverse_factors([mul_tn(first, first)], factor_ref)
     transfer = mul_nt(first, factor)
     transfer_ref[...] = transfer
     coefs = mul_tn(transfer, stacked[:, rank:])
@@ -304,6 +348,7 @@
     full_recv,
     root_send,
     root_recv,
+    factor_ref,
 ):
     rank = coef_ref.shape[0]
     count = mids * GROUP
@@ -361,7 +406,7 @@
     for copy in copies:
         copy.wait()
 
-    (factor,) = inverse_factors([full_ref[:rank]])
+    (factor,) = inverse_factors([full_ref[:rank]], factor_ref)
     own = mul_nn(factor, full_ref[rank:])
     own_ref[...] = own
     copies = []
@@ -382,7 +427,7 @@
         copy.wait()
         other = other_ref[step]
         gram = gram + mul_tn(other, other)
-    (factor,) = inverse_factors([gram])
+    (factor,) = inverse_factors([gram], factor_ref)
     share_rows = rank // GROUP
     mine = jnp.zeros((share_rows, rank), F32)
     for place in range(GROUP):
@@ -436,7 +481,10 @@
             pltpu.VMEM((2 * proxies, 2 * rank), BF16),
             pltpu.VMEM((ROW_CHUNK, 2 * proxies), BF16),
             pltpu.VMEM((ROW_CHUNK, 2 * proxies), BF16),
+            pltpu.VMEM((ROW_CHUNK, 2 * proxies), BF16),
+            pltpu.VMEM((ROW_CHUNK, 2 * proxies), BF16),
             pltpu.VMEM((4, leaves * leaf_rows, rank), F32),
+            pltpu.VMEM((leaves, 2, ROWS8 + 1, ROWS8, rank), F32),
         ],
         compiler_params=pltpu.CompilerParams(vmem_limit_bytes=limit),
         name="leaf_and_node",
@@ -462,6 +510,7 @@
             dma((GROUP,)),
             dma((mids,)),
             dma((mids,)),
+            pltpu.VMEM((1, 2, ROWS8 + 1, ROWS8, rank), F32),
         ],
         compiler_params=pltpu.CompilerParams(
             collective_id=1, has_side_effects=True, vmem_limit_bytes=limit

time: 81.7 us -> 68.9 us (0.84)
  Pallas kernels: 76.2 us -> 63.4 us
    pallas_call x1, Pallas kernels: 35.9 us -> 29.1 us  [on_device(): pl.pallas_call(functools.partial(leaf_kernel, per_dev), out_shape=(jax.Sh...]
    pallas_call x1, Pallas kernels: 29.8 us -> 23.8 us  [on_device(): pl.pallas_call(functools.partial(tree_kernel, mids), out_shape=(jax.Shape...]
where the time goes in v1:
time: 68.9 us; the launch traced here: 68.6 us
  Pallas kernels  63.4 us (92%)
  local copies, waits for them, and re-layouts  3.2 us (5%)
  between operations  2.05 us (3%)
    pallas_call x1, Pallas kernels, on_device(): pl.pallas_call(functools.partial(leaf_kernel, per_dev), out_shape=(jax.Sh...  29.1 us
    pallas_call x1, Pallas kernels, on_device(): pl.pallas_call(functools.partial(tree_kernel, mids), out_shape=(jax.Shape...  23.8 us
    pallas_call x1, Pallas kernels, on_device(): pl.pallas_call(functools.partial(gather_kernel, count), out_shape=jax.Sha...  10.4 us
    unnamed x14, local copies, waits for them, and re-layouts  2.48 us

profile of v1, /device:TPU:0, one launch (start us, length us, event | category | flops | bytes accessed | tf_op | source)
XLA Modules:
  0.0 68.6 jit_solution(5526682784090746135)
XLA Ops:
  0.6 0.7 %reshape.14 = f32[3,4,128]{2,1,0:T(4,128)S(1)} reshape(f32[3,512]{1,0:T(4,128)} %param.9) | data formatting | bytes 12288 | tf_op jit(solution)/shard_map/reshape | solution.py:453
  1.4 0.0 copy-start.1
  1.4 0.0 copy-start.2
  1.4 0.0 copy-start.4
  1.4 0.0 copy-start.5
  1.4 10.4 %gather_centroids.1 = f32[3,16,8,128]{3,2,1,0:T(8,128)S(1)} custom-call(f32[3,8,128]{2,1,0:T(8,128)S(1)} %pad.4.own_ref), custom_call_target="tpu_custom_call" | custom-call | tf_op jit(solution)/shard_map/gather_centroids/pallas_call | solution.py:455
  11.8 0.0 copy-start.3
  12.5 0.0 copy-done.1
  12.5 0.0 copy-done.2
  12.5 0.0 copy-done.4
  12.5 0.0 copy-done.5
  12.5 0.0 copy-done.3
  12.6 0.0 copy-start
  12.6 1.2 %copy-done = f32[2048,128]{1,0:T(8,128)S(1)} copy-done((f32[2048,128]{1,0:T(8,128)S(1)}, f32[2048,128]{1,0:T(8,128)}, u32[]{:S(2)}) %copy-start) | copy-done | bytes 1048600
  13.8 29.1 %leaf_and_node.1 = (f32[2,256,128]{2,1,0:T(8,128)}, f32[256,128]{1,0:T(8,128)}, f32[128,128]{1,0:T(8,128)S(1)}, f32[256,128]{1,0:T(8,128)S(1)}) custom-call(f32[1]{0:T(128)S(6)} %copy.16.kappa_ref, f32[3,128,128]{2,1,0:T(8,128)S(1)} %bitcast.7, s32[2,256]{1,0:T(2,128)S(1)} %copy-done.5, s32[2,1024]{1,0:T(2,128)S(1)} %copy-done.1, s32[1,1024]{1,0:T(1,128)S(1)} %copy-done.3, ...), custom_call_target="tpu_custom_call" | custom-call | tf_op jit(solution)/shard_map/leaf_and_node/pallas_call | solution.py:468
  43.5 23.8 %mid_and_root.1 = (f32[128,128]{1,0:T(8,128)S(1)}, f32[16,128]{1,0:T(8,128)S(1)}) custom-call(s32[16,128]{1,0:T(8,128)S(1)} %broadcast_in_dim.17.pos_ref, f32[128,128]{1,0:T(8,128)S(1)} %get-tuple-element.12.coef_ref, f32[256,128]{1,0:T(8,128)S(1)} %get-tuple-element.13.sums_ref), custom_call_target="tpu_custom_call" | custom-call | tf_op jit(solution)/shard_map/mid_and_root/pallas_call | solution.py:494
  67.4 0.6 copy.17
  68.0 0.6 copy.18
  (2 shorter events, 0.0 us)
Async XLA Ops:
  1.4 11.2 %copy-start.1 = (s32[2,1024]{1,0:T(2,128)S(1)}, s32[2,1024]{1,0:T(2,128)}, u32[]{:S(2)}) copy-start(s32[2,1024]{1,0:T(2,128)} %leaf_proxy_ref.1) | copy-start | bytes 24580
  1.4 11.2 %copy-start.2 = (s32[2,1024]{1,0:T(2,128)S(1)}, s32[2,1024]{1,0:T(2,128)}, u32[]{:S(2)}) copy-start(s32[2,1024]{1,0:T(2,128)} %mid_proxy_ref.1) | copy-start | bytes 24580
  1.4 11.2 %copy-start.4 = (s32[1024]{0:T(1024)S(1)}, s32[1024]{0:T(1024)}, u32[]{:S(2)}) copy-start(s32[1024]{0:T(1024)} %param.14) | copy-start | bytes 12292
  1.4 11.2 %copy-start.5 = (s32[2,256]{1,0:T(2,128)S(1)}, s32[2,256]{1,0:T(2,128)}, u32[]{:S(2)}) copy-start(s32[2,256]{1,0:T(2,128)} %leaf_tri_ref.1) | copy-start | bytes 6148
  11.8 0.7 %copy-start.3 = (s32[1,1024]{1,0:T(1,128)S(1)}, s32[1,1024]{1,0:T(1,128)}, u32[]{:S(2)}) copy-start(s32[1,1024]{1,0:T(1,128)} %node_proxy_ref.1) | copy-start | bytes 12292
  12.6 1.2 %copy-start = (f32[2048,128]{1,0:T(8,128)S(1)}, f32[2048,128]{1,0:T(8,128)}, u32[]{:S(2)}) copy-start(f32[2048,128]{1,0:T(8,128)} %omega_ref.1) | copy-start | bytes 3145732

commit v2 on v1

--- a/solution.py
+++ b/solution.py
@@ -18,18 +18,18 @@
 BF16 = jnp.bfloat16
 
 SIN_COEF = (
-    3.141592640130707,
-    -5.167710083507899,
-    2.5500775232144695,
-    -0.5982912856189484,
-    0.07765766030176967,
+    4.442882919124344,
+    -7.30824568650907,
+    3.606354218432694,
+    -0.846111650371952,
+    0.10982451642092537,
 )
 COS_COEF = (
-    1.9999999064952165,
-    -9.8695856612393,
-    8.116822705725152,
-    -2.6637531361606688,
-    0.43937922219243786,
+    1.4142134962552284,
+    -6.978850948563824,
+    5.7394603769071955,
+    -1.8835579059861416,
+    0.31068802752474356,
 )
 
 
@@ -141,14 +141,14 @@
         return carry
 
     lax.fori_loop(1, count, greet, 0)
-    local = pltpu.make_async_copy(own_ref, table_ref.at[:, me], local_sem)
+    local = pltpu.make_async_copy(own_ref, table_ref.at[me], local_sem)
     local.start()
     pl.semaphore_wait(barrier, count - 1)
 
     def copy_of(step):
         return pltpu.make_async_remote_copy(
             src_ref=own_ref,
-            dst_ref=table_ref.at[:, me],
+            dst_ref=table_ref.at[me],
             send_sem=send_sem.at[step],
             recv_sem=recv_sem.at[step],
             device_id={"sub": lax.rem(me + step, count)},
@@ -198,32 +198,38 @@
     rank = omega_ref.shape[1]
     rows = leaves * leaf_rows
 
+    turns = kappa_ref[0] * (0.5 / math.pi)
+    soft = turns * turns * soft_sq
+    per_axis = per_dev // LANES
+    blocks = table_ref.shape[0] * ROWS8
     pieces = []
-    for axis in range(3):
-        turned = table_ref[axis].T
+    for tile in range(table_ref.shape[1] // ROWS8):
+        turned = table_ref[:, tile * ROWS8 : (tile + 1) * ROWS8, :].reshape(blocks, LANES).T
         first = turned.astype(BF16)
         left = turned - first.astype(F32)
         second = left.astype(BF16)
         third = (left - second.astype(F32)).astype(BF16)
         pieces.append((first, second, third))
-    blocks = table_ref.shape[1]
 
     def centroids(index):
         width = index.shape[1]
-        within = index % per_dev
-        block = (index // per_dev) * ROWS8 + within // LANES
-        place = within % LANES
-        hot = jnp.where(
-            lax.broadcasted_iota(jnp.int32, (blocks, width), 0) == block, 1.0, 0.0
-        ).astype(BF16)
+        within = index & (per_dev - 1)
+        block = (index >> (per_dev.bit_length() - 1)) * ROWS8 + (within >> 7)
+        place = index & (LANES - 1)
+        block_row = lax.broadcasted_iota(jnp.int32, (blocks, width), 0)
+        hot = {
+            offset: jnp.where(block_row == block + offset, 1.0, 0.0).astype(BF16)
+            for offset in range(0, ROWS8, per_axis)
+        }
         chosen = lax.broadcasted_iota(jnp.int32, (LANES, width), 0) == place
         found = []
         for axis in range(3):
             wide = None
-            for piece in pieces[axis]:
-                term = jnp.dot(piece, hot, preferred_element_type=F32)
+            tile, offset = divmod(axis * per_axis, ROWS8)
+            for piece in pieces[tile]:
+                term = jnp.dot(piece, hot[offset], preferred_element_type=F32)
                 wide = term if wide is None else wide + term
-            found.append(jnp.sum(jnp.where(chosen, wide, 0.0), axis=0, keepdims=True))
+            found.append(jnp.sum(jnp.where(chosen, wide, 0.0), axis=0, keepdims=True) * turns)
         return found
 
     group = device // GROUP
@@ -241,11 +247,10 @@
                 turned[:, axis : axis + 1], (leaf_rows, rows_ref.shape[2])
             )
 
-    omega_high, omega_low = split(omega_ref[...])
+    omega_high, omega_low = split(omega_ref[...] * turns)
     weight_ref[:, :rank] = omega_high
     weight_ref[:, rank:] = omega_low
 
-    turns = kappa_ref[0] * (0.5 / math.pi)
     chunks = rows // ROW_CHUNK
     per_leaf = leaf_rows // ROW_CHUNK
     width = rows_ref.shape[2]
@@ -268,16 +273,15 @@
                 for axis in range(3):
                     apart = mine[axis] - cols_ref[number, axis : axis + 1, begin : begin + width]
                     squared = apart * apart if squared is None else squared + apart * apart
-                squared = squared + soft_sq
+                squared = squared + soft
                 inverse = lax.rsqrt(squared)
-                phase = (squared * inverse) * turns
+                phase = squared * inverse
                 phase = phase - jnp.round(phase)
                 square = phase * phase
                 sine = phase * poly(SIN_COEF, square)
                 twice = poly(COS_COEF, square)
                 imag = (sine * twice) * inverse
-                sine = sine * sine
-                real = (1.0 - (sine + sine)) * inverse
+                real = (1.0 - sine * sine) * inverse
                 for value, offset in ((real, 0), (imag, proxies)):
                     high, low = split(value)
                     high_refs[slot][top : top + 16, offset + begin : offset + begin + width] = high
@@ -450,11 +454,11 @@
     dma = pltpu.SemaphoreType.DMA
     limit = 48 * 1024 * 1024
 
-    own = tri_xyz.reshape(3, per_dev // LANES, LANES)
-    own = jnp.pad(own, ((0, 0), (0, ROWS8 - per_dev // LANES), (0, 0)))
+    own = tri_xyz.reshape(3 * per_dev // LANES, LANES)
+    own = jnp.pad(own, ((0, -own.shape[0] % ROWS8), (0, 0)))
     table = pl.pallas_call(
         functools.partial(gather_kernel, count),
-        out_shape=jax.ShapeDtypeStruct((3, count, ROWS8, LANES), F32),
+        out_shape=jax.ShapeDtypeStruct((count,) + own.shape, F32),
         in_specs=[vmem],
         out_specs=vmem,
         scratch_shapes=[dma((count,)), dma((count,)), dma],
@@ -463,7 +467,6 @@
         ),
         name="gather_centroids",
     )(own)
-    table = table.reshape(3, count * ROWS8, LANES)
 
     basis, transfer, coef, sums = pl.pallas_call(
         functools.partial(leaf_kernel, per_dev),

time: 68.9 us -> 67 us (0.972)
  Pallas kernels: 63.4 us -> 61.5 us
    pallas_call x1, Pallas kernels: 10.4 us -> 9.6 us  [on_device(): pl.pallas_call(functools.partial(gather_kernel, count), out_shape=jax.Sha...]
where the time goes in v2:
time: 67 us; the launch traced here: 66.7 us
  Pallas kernels  61.5 us (92%)
  local copies, waits for them, and re-layouts  3.2 us (5%)
  between operations  2.05 us (3%)
    pallas_call x1, Pallas kernels, on_device(): pl.pallas_call(functools.partial(leaf_kernel, per_dev), out_shape=(jax.Sh...  28.5 us
    pallas_call x1, Pallas kernels, on_device(): pl.pallas_call(functools.partial(tree_kernel, mids), out_shape=(jax.Shape...  23.4 us
    pallas_call x1, Pallas kernels, on_device(): pl.pallas_call(functools.partial(gather_kernel, count), out_shape=jax.Sha...  9.6 us
    unnamed x14, local copies, waits for them, and re-layouts  2.48 us

profile of v2, /device:TPU:0, one launch (start us, length us, event | category | flops | bytes accessed | tf_op | source)
XLA Modules:
  0.0 66.7 jit_solution(7118557328754369836)
XLA Ops:
  0.6 0.7 %reshape.11 = f32[12,128]{1,0:T(8,128)S(1)} reshape(f32[3,512]{1,0:T(4,128)} %param.9) | data formatting | bytes 12288 | tf_op jit(solution)/shard_map/reshape | solution.py:457
  1.3 0.0 copy-start.1
  1.4 0.0 copy-start.2
  1.4 0.0 copy-start.3
  1.4 0.0 copy-start.4
  1.4 9.6 %gather_centroids.1.table_ref = f32[16,16,128]{2,1,0:T(8,128)S(1)} custom-call(f32[16,128]{1,0:T(8,128)S(1)} %pad.4.own_ref), custom_call_target="tpu_custom_call" | custom-call | tf_op jit(solution)/shard_map/gather_centroids/pallas_call | solution.py:459
  11.0 0.0 copy-start.5
  11.7 0.0 copy-done.1
  11.7 0.0 copy-done.2
  11.7 0.0 copy-done.3
  11.7 0.0 copy-done.4
  11.7 0.0 copy-done.5
  11.7 0.0 copy-start
  11.7 1.2 %copy-done = f32[2048,128]{1,0:T(8,128)S(1)} copy-done((f32[2048,128]{1,0:T(8,128)S(1)}, f32[2048,128]{1,0:T(8,128)}, u32[]{:S(2)}) %copy-start) | copy-done | bytes 1048600
  12.9 28.5 %leaf_and_node.1 = (f32[2,256,128]{2,1,0:T(8,128)}, f32[256,128]{1,0:T(8,128)}, f32[128,128]{1,0:T(8,128)S(1)}, f32[256,128]{1,0:T(8,128)S(1)}) custom-call(f32[1]{0:T(128)S(6)} %copy.16.kappa_ref, f32[16,16,128]{2,1,0:T(8,128)S(1)} %gather_centroids.1.table_ref, s32[2,256]{1,0:T(2,128)S(1)} %copy-done.5, s32[2,1024]{1,0:T(2,128)S(1)} %copy-done.1, ...), custom_call_target="tpu_custom_call" | custom-call | tf_op jit(solution)/shard_map/leaf_and_node/pallas_call | solution.py:471
  42.1 23.4 %mid_and_root.1 = (f32[128,128]{1,0:T(8,128)S(1)}, f32[16,128]{1,0:T(8,128)S(1)}) custom-call(s32[16,128]{1,0:T(8,128)S(1)} %broadcast_in_dim.17.pos_ref, f32[128,128]{1,0:T(8,128)S(1)} %get-tuple-element.12.coef_ref, f32[256,128]{1,0:T(8,128)S(1)} %get-tuple-element.13.sums_ref), custom_call_target="tpu_custom_call" | custom-call | tf_op jit(solution)/shard_map/mid_and_root/pallas_call | solution.py:497
  65.5 0.6 copy.17
  66.1 0.6 copy.18
  (2 shorter events, 0.0 us)
Async XLA Ops:
  1.3 10.3 %copy-start.1 = (s32[2,1024]{1,0:T(2,128)S(1)}, s32[2,1024]{1,0:T(2,128)}, u32[]{:S(2)}) copy-start(s32[2,1024]{1,0:T(2,128)} %leaf_proxy_ref.1) | copy-start | bytes 24580
  1.4 10.3 %copy-start.2 = (s32[2,1024]{1,0:T(2,128)S(1)}, s32[2,1024]{1,0:T(2,128)}, u32[]{:S(2)}) copy-start(s32[2,1024]{1,0:T(2,128)} %mid_proxy_ref.1) | copy-start | bytes 24580
  1.4 10.3 %copy-start.3 = (s32[1,1024]{1,0:T(1,128)S(1)}, s32[1,1024]{1,0:T(1,128)}, u32[]{:S(2)}) copy-start(s32[1,1024]{1,0:T(1,128)} %node_proxy_ref.1) | copy-start | bytes 12292
  1.4 10.3 %copy-start.4 = (s32[1024]{0:T(1024)S(1)}, s32[1024]{0:T(1024)}, u32[]{:S(2)}) copy-start(s32[1024]{0:T(1024)} %param.14) | copy-start | bytes 12292
  11.0 0.7 %copy-start.5 = (s32[2,256]{1,0:T(2,128)S(1)}, s32[2,256]{1,0:T(2,128)}, u32[]{:S(2)}) copy-start(s32[2,256]{1,0:T(2,128)} %leaf_tri_ref.1) | copy-start | bytes 6148
  11.7 1.2 %copy-start = (f32[2048,128]{1,0:T(8,128)S(1)}, f32[2048,128]{1,0:T(8,128)}, u32[]{:S(2)}) copy-start(f32[2048,128]{1,0:T(8,128)} %omega_ref.1) | copy-start | bytes 3145732
